TPU v7x, 32 devices: a whole 2x2x4 slice. The times are simulated.
32 devices in a mesh: grp: 4 (over x, core), wide: 8 (over z, y).
Axes of the slice: x: 2, y: 2, z: 4, core: 2. Of those that a mesh axis runs over, the one named last changes fastest.
Arguments:
- anchor_states: bfloat16 [4096, 1024], P(('wide', 'grp')), may hold values from -6 to 6
- key_weight: bfloat16 [1024, 1024], P(None, 'grp'), may hold values from -0.1875 to 0.1875
- value_weight: bfloat16 [1024, 1024], P(None, 'grp'), may hold values from -0.1875 to 0.1875
- panel_query: bfloat16 [8192, 1024], P(('wide', 'grp')), may hold values from -160 to 160
- cell_list: int32 [64, 4], P('wide'), may hold values from 0 to 3, as said below
- cell_count: int32 [64], P('wide'), may hold values from 1 to 4, as said below
- norm_gain: float32 [1024], replicated, may hold values from 0.1 to 1.9
- up_weight: bfloat16 [1024, 512], replicated, may hold values from -0.1875 to 0.1875
- flux_weight: bfloat16 [4, 512], replicated, may hold values from -0.25 to 0.25
Outputs:
- flux: float32 [4, 8192], P(None, ('wide', 'grp'))
Inputs may be any that keep to these rules, and one draw needn't show every extreme that they name: `cell_list`: the entries of a row are distinct cell blocks of that panel block's region; entries past cell_count are not used. `cell_count`: every region has a panel block whose list uses all 4 slots.
All inputs are finite; a program needn't handle non-finite values.
Results may differ from a plain program's by a relative error of at most 0.007.
Values may be sent and summed in bfloat16 or wider, within the bound.
A program may use at most 64 MiB of HBM per device.

v0:
```python
import math

import jax
import jax.numpy as jnp
from jax import lax
from jax.sharding import PartitionSpec as P

BLK = 128
LMAX = 4
HD = 64


def softmax_rows(scores, mask):
    scores = jnp.where(mask[:, None, None, :], scores, -jnp.inf)
    top = jnp.max(scores, axis=-1, keepdims=True)
    expo = jnp.exp(scores - top)
    return (expo / jnp.sum(expo, axis=-1, keepdims=True)).astype(jnp.bfloat16)


def wall_flux(query_rows, attended_rows, norm_gain, up_weight, flux_weight):
    stream = query_rows.astype(jnp.float32) + attended_rows.astype(jnp.float32)
    scale = lax.rsqrt(jnp.mean(stream * stream, axis=-1, keepdims=True) + 1e-06)
    normed = (stream * scale * norm_gain[None, :]).astype(jnp.bfloat16)
    hidden = jax.nn.gelu(jnp.dot(normed, up_weight, preferred_element_type=jnp.float32)).astype(
        jnp.bfloat16
    )
    return lax.dot_general(
        flux_weight, hidden, (((1,), (1,)), ((), ())), preferred_element_type=jnp.float32
    )


def body(
    anchor_states,
    key_weight,
    value_weight,
    panel_query,
    cell_list,
    cell_count,
    norm_gain,
    up_weight,
    flux_weight,
):
    full_keys_w, full_values_w = (
        lax.all_gather(key_weight, "grp", axis=1, tiled=True),
        lax.all_gather(value_weight, "grp", axis=1, tiled=True),
    )
    local_keys = jnp.dot(anchor_states, full_keys_w, preferred_element_type=jnp.float32).astype(
        jnp.bfloat16
    )
    local_values = jnp.dot(anchor_states, full_values_w, preferred_element_type=jnp.float32).astype(
        jnp.bfloat16
    )
    region_keys, region_values = (
        lax.all_to_all(local_keys, "grp", split_axis=1, concat_axis=0, tiled=True),
        lax.all_to_all(local_values, "grp", split_axis=1, concat_axis=0, tiled=True),
    )
    region_query = lax.all_to_all(
        lax.all_to_all(panel_query, "grp", split_axis=1, concat_axis=0, tiled=True),
        "wide",
        split_axis=0,
        concat_axis=0,
        tiled=True,
    )
    local_heads = region_keys.shape[1] // HD
    cell_blocks = region_keys.shape[0] // BLK
    block_count = region_query.shape[0] // BLK
    per_step = math.gcd(block_count, 4)
    steps = block_count // per_step
    key_blocks = region_keys.reshape(cell_blocks, BLK, local_heads, HD)
    value_blocks = region_values.reshape(cell_blocks, BLK, local_heads, HD)
    query_groups = region_query.reshape(steps, per_step, BLK, local_heads, HD)
    list_groups = cell_list.reshape(steps, per_step, LMAX)
    count_groups = cell_count.reshape(steps, per_step)
    slot_index = jnp.arange(LMAX, dtype=jnp.int32)

    def attend(item):
        query_group, listed, counts = item
        live = slot_index[None, :] < counts[:, None]
        picked_keys = key_blocks[listed].reshape(per_step, LMAX * BLK, local_heads, HD)
        picked_values = value_blocks[listed].reshape(per_step, LMAX * BLK, local_heads, HD)
        mask = jnp.repeat(live, BLK, axis=1)
        scores = jnp.einsum(
            "bihd,bjhd->bhij", query_group, picked_keys, preferred_element_type=jnp.float32
        ) / math.sqrt(HD)
        weights = softmax_rows(scores, mask)
        output = jnp.einsum(
            "bhij,bjhd->bihd", weights, picked_values, preferred_element_type=jnp.float32
        )
        return output.astype(jnp.bfloat16)

    attended = lax.map(attend, (query_groups, list_groups, count_groups))
    attended = attended.reshape(block_count * BLK, local_heads * HD)
    panel_rows = lax.all_to_all(
        lax.all_to_all(attended, "wide", split_axis=0, concat_axis=0, tiled=True),
        "grp",
        split_axis=0,
        concat_axis=1,
        tiled=True,
    )
    return wall_flux(panel_query, panel_rows, norm_gain, up_weight, flux_weight)


def solution(mesh):
    in_specs = (
        P(("wide", "grp"), None),
        P(None, "grp"),
        P(None, "grp"),
        P(("wide", "grp"), None),
        P("wide", None),
        P("wide"),
        P(),
        P(),
        P(),
    )
    out_specs = P(None, ("wide", "grp"))
    return jax.shard_map(body, mesh=mesh, in_specs=in_specs, out_specs=out_specs, check_vma=False)
```

profile of v0, /device:TPU:0, one launch (start us, length us, event | category | flops | bytes accessed | tf_op | source)
XLA Modules:
  0.0 153.0 jit_solution(880974566185352678)
XLA Ops:
  6.5 0.7 all-gather.3.cloned.1.call-update
  7.3 0.0 all-gather.5.cloned.1.call-start
  7.3 0.7 all-gather.5.cloned.1.call-update
  8.0 1.3 copy.26
  9.3 13.9 %all_to_all.79 = bf16[256,4,256]{0,2,1:T(8,128)(2,1)S(1)} all-to-all(bf16[256,4,256]{0,2,1:T(8,128)(2,1)S(1)} %bitcast.72), channel_id=1, replica_groups=mesh['grp'=4,'wide'=8] {'grp'}, dimensions={1} | all-to-all | bytes 1048576 | tf_op jit(solution)/shard_map/all_to_all | solution.py:58
  23.2 1.0 copy.29
  24.2 6.2 %all-to-all-start.2 = ((bf16[8,128,256]{2,1,0:T(8,128)(2,1)}), bf16[8,128,256]{2,1,0:T(8,128)(2,1)S(1)}, u32[]{:S(2)}, u32[]{:S(2)}) async-start(bf16[8,128,256]{2,1,0:T(8,128)(2,1)} %bitcast.6), calls=%async_computation.2 | async-start | bytes 1048576 | tf_op jit(solution)/shard_map/all_to_all | solution.py:57
  30.4 4.8 %all-gather.3.cloned.1.call-done = bf16[1024,1024]{1,0:T(8,128)(2,1)} async-done(((bf16[1024,256]{1,0:T(8,128)(2,1)}), bf16[1024,1024]{1,0:T(8,128)(2,1)}) %all-gather.3.cloned.1.call-update) | async-done | bytes 2097168 | tf_op jit(solution)/shard_map/all_gather | solution.py:45
  35.2 2.0 %convolution_convert_fusion.1 = bf16[128,1024]{1,0:T(8,128)(2,1)S(1)} fusion(bf16[128,1024]{1,0:T(8,128)(2,1)S(1)} %copy-done.1, bf16[1024,1024]{1,0:T(8,128)(2,1)} %all-gather.3.cloned.1.call-done), kind=kOutput, calls=%fused_computation.31 | convolution fusion | flops 268566528 | bytes 2621440 | tf_op jit(solution)/shard_map/dot_general | solution.py:50
  37.2 0.8 copy.38
  38.1 6.2 %all-to-all-done.2 = bf16[8,128,256]{2,1,0:T(8,128)(2,1)S(1)} async-done(((bf16[8,128,256]{2,1,0:T(8,128)(2,1)}), bf16[8,128,256]{2,1,0:T(8,128)(2,1)S(1)}, u32[]{:S(2)}, u32[]{:S(2)}) %all-to-all-start.2) | async-done | bytes 524320 | tf_op jit(solution)/shard_map/all_to_all | solution.py:57
  44.2 3.5 %all-to-all-start = ((bf16[128,4,256]{0,2,1:T(8,128)(2,1)}), bf16[128,4,256]{0,2,1:T(8,128)(2,1)S(1)}, u32[]{:S(2)}, u32[]{:S(2)}) async-start(bf16[128,4,256]{0,2,1:T(8,128)(2,1)} %bitcast.1), calls=%async_computation | async-start | bytes 524288 | tf_op jit(solution)/shard_map/all_to_all | solution.py:55
  47.8 15.0 %all-gather.5.cloned.1.call-done = bf16[1024,1024]{1,0:T(8,128)(2,1)} async-done(((bf16[1024,256]{1,0:T(8,128)(2,1)}), bf16[1024,1024]{1,0:T(8,128)(2,1)}) %all-gather.5.cloned.1.call-update) | async-done | bytes 2097168 | tf_op jit(solution)/shard_map/all_gather | solution.py:44
  62.7 2.0 %convolution_convert_fusion = bf16[128,1024]{1,0:T(8,128)(2,1)S(1)} fusion(bf16[128,1024]{1,0:T(8,128)(2,1)S(1)} %copy-done.1, bf16[1024,1024]{1,0:T(8,128)(2,1)} %all-gather.5.cloned.1.call-done), kind=kOutput, calls=%fused_computation.30 | convolution fusion | flops 268566528 | bytes 2621440 | tf_op jit(solution)/shard_map/dot_general | solution.py:47
  64.8 0.8 copy.39
  65.6 3.4 %all-to-all-start.3 = ((bf16[128,4,256]{0,2,1:T(8,128)(2,1)}), bf16[128,4,256]{0,2,1:T(8,128)(2,1)S(1)}, u32[]{:S(2)}, u32[]{:S(2)}) async-start(bf16[128,4,256]{0,2,1:T(8,128)(2,1)} %bitcast.8), calls=%async_computation.3 | async-start | bytes 524288 | tf_op jit(solution)/shard_map/all_to_all | solution.py:54
  69.1 0.1 copy.37
  69.1 0.1 reshape.92
  69.2 0.3 copy.30
  69.5 0.3 copy.33
  69.8 5.2 %all-to-all-done.3 = bf16[128,4,256]{0,2,1:T(8,128)(2,1)S(1)} async-done(((bf16[128,4,256]{0,2,1:T(8,128)(2,1)}), bf16[128,4,256]{0,2,1:T(8,128)(2,1)S(1)}, u32[]{:S(2)}, u32[]{:S(2)}) %all-to-all-start.3) | async-done | bytes 262176 | tf_op jit(solution)/shard_map/all_to_all | solution.py:54
  75.0 0.3 copy.34
  75.4 34.9 %while.11 = (s32[]{:T(128)}, bf16[2,4,128,4,64]{2,4,3,1,0:T(8,128)(2,1)}, s32[2,4,4]{2,1,0:T(4,128)S(1)}, bf16[4,128,4,64]{3,2,1,0:T(4,128)(2,1)S(1)}, s32[2,4]{...) while((s32[]{:T(128)}, ...), condition=%wide.region_3.4_spmd.clone, body=%wide.region_0.3_spmd.clone.sunk | while | flops 276956736 | bytes 24671344 | solution.py:91
  75.4 0.1 reshape.132
  75.5 3.6 %gather_fusion = bf16[16,128,4,64]{3,2,1,0:T(4,128)(2,1)} fusion(bf16[4,128,4,64]{3,2,1,0:T(4,128)(2,1)S(1)} %get-tuple-element.170, s32[1024]{0:T(1024)S(1)} %pad_clamp_fusion.2), kind=kCustom, calls=%fused_computation.1.clone.clone.1 | custom fusion | bytes 2097216 | tf_op jit(solution)/shard_map/while/body/eval_jaxpr/gather | solution.py:79
  79.0 2.4 %fusion.59 = f32[4,4,128,512]{3,2,1,0:T(8,128)S(1)} fusion(bf16[4,512,4,64]{3,2,1,0:T(4,128)(2,1)} %bitcast.70, bf16[2,4,128,4,64]{2,4,3,1,0:T(8,128)(2,1)S(1)} %get-tuple-element.169, s32[]{:T(128)} %get-tuple-element.156), kind=kOutput, calls=%fused_computation.10.clone.1 | convolution fusion | flops 134217728 | bytes 5505028 | tf_op jit(solution)/shard_map/while/body/eval_jaxpr/bihd,bjhd->bhij/dot_general | solution.py:82
  81.4 0.1 iota_compare_fusion.2
  81.5 0.1 broadcast_bitcast_fusion.2
  81.6 3.0 %fusion.61 = (f32[4,4,128]{2,1,0:T(4,128)S(1)}, f32[4,4,128,512]{3,2,1,0:T(8,128)}) fusion(f32[4,4,128,512]{3,2,1,0:T(8,128)S(1)} %fusion.59, pred[4,512]{1,0:T(4,128)(4,1)S(1)} %bitcast.79), kind=kOutput, calls=%fused_computation.51.clone.1 | output fusion | flops 6291967 | bytes 8398848 | tf_op jit(solution)/shard_map/while/body/eval_jaxpr/sub | solution.py:16
  84.6 3.6 %gather_fusion.1 = bf16[16,128,4,64]{3,2,1,0:T(4,128)(2,1)} fusion(bf16[4,128,4,64]{3,2,1,0:T(4,128)(2,1)S(1)} %get-tuple-element.167, s32[1024]{0:T(1024)S(1)} %pad_clamp_fusion.2), kind=kCustom, calls=%fused_computation.clone.clone.1 | custom fusion | bytes 2097216 | tf_op jit(solution)/shard_map/while/body/eval_jaxpr/gather | solution.py:80
  88.2 4.6 %fusion.62 = bf16[2,4,128,4,64]{2,4,3,1,0:T(8,128)(2,1)} fusion(bf16[2,4,128,4,64]{2,4,3,1,0:T(8,128)(2,1)} %get-tuple-element.157, s32[]{:T(128)} %get-tuple-element.156, f32[4,4,128,512]{3,2,1,0:T(8,128)} %get-tuple-element.146, f32[4,4,128]{2,1,0:T(4,128)S(1)} %get-tuple-element.147, bf16[4,512,4,64]{3,2,1,0:T(4,128)(2,1)} %bitcast.71), kind=kOutput, calls=%fused_computation.17.clone.1 | convolution fusion | flops 136445952 | bytes 6562304 | tf_op jit(solution)/shard_map/while/body/eval_jaxpr/bhij,bjhd->bihd/dot_general | solution.py:86
  92.8 0.1 reshape.132
  92.9 3.6 %gather_fusion = bf16[16,128,4,64]{3,2,1,0:T(4,128)(2,1)} fusion(bf16[4,128,4,64]{3,2,1,0:T(4,128)(2,1)S(1)} %get-tuple-element.170, s32[1024]{0:T(1024)S(1)} %pad_clamp_fusion.2), kind=kCustom, calls=%fused_computation.1.clone.clone.1 | custom fusion | bytes 2097216 | tf_op jit(solution)/shard_map/while/body/eval_jaxpr/gather | solution.py:79
  96.5 2.4 %fusion.59 = f32[4,4,128,512]{3,2,1,0:T(8,128)S(1)} fusion(bf16[4,512,4,64]{3,2,1,0:T(4,128)(2,1)} %bitcast.70, bf16[2,4,128,4,64]{2,4,3,1,0:T(8,128)(2,1)S(1)} %get-tuple-element.169, s32[]{:T(128)} %get-tuple-element.156), kind=kOutput, calls=%fused_computation.10.clone.1 | convolution fusion | flops 134217728 | bytes 5505028 | tf_op jit(solution)/shard_map/while/body/eval_jaxpr/bihd,bjhd->bhij/dot_general | solution.py:82
  98.9 0.1 iota_compare_fusion.2
  99.0 0.1 broadcast_bitcast_fusion.2
  99.0 3.0 %fusion.61 = (f32[4,4,128]{2,1,0:T(4,128)S(1)}, f32[4,4,128,512]{3,2,1,0:T(8,128)}) fusion(f32[4,4,128,512]{3,2,1,0:T(8,128)S(1)} %fusion.59, pred[4,512]{1,0:T(4,128)(4,1)S(1)} %bitcast.79), kind=kOutput, calls=%fused_computation.51.clone.1 | output fusion | flops 6291967 | bytes 8398848 | tf_op jit(solution)/shard_map/while/body/eval_jaxpr/sub | solution.py:16
  102.1 3.6 %gather_fusion.1 = bf16[16,128,4,64]{3,2,1,0:T(4,128)(2,1)} fusion(bf16[4,128,4,64]{3,2,1,0:T(4,128)(2,1)S(1)} %get-tuple-element.167, s32[1024]{0:T(1024)S(1)} %pad_clamp_fusion.2), kind=kCustom, calls=%fused_computation.clone.clone.1 | custom fusion | bytes 2097216 | tf_op jit(solution)/shard_map/while/body/eval_jaxpr/gather | solution.py:80
  105.6 4.6 %fusion.62 = bf16[2,4,128,4,64]{2,4,3,1,0:T(8,128)(2,1)} fusion(bf16[2,4,128,4,64]{2,4,3,1,0:T(8,128)(2,1)} %get-tuple-element.157, s32[]{:T(128)} %get-tuple-element.156, f32[4,4,128,512]{3,2,1,0:T(8,128)} %get-tuple-element.146, f32[4,4,128]{2,1,0:T(4,128)S(1)} %get-tuple-element.147, bf16[4,512,4,64]{3,2,1,0:T(4,128)(2,1)} %bitcast.71), kind=kOutput, calls=%fused_computation.17.clone.1 | convolution fusion | flops 136445952 | bytes 6562304 | tf_op jit(solution)/shard_map/while/body/eval_jaxpr/bhij,bjhd->bihd/dot_general | solution.py:86
  110.3 19.8 %all_to_all.80 = bf16[8,128,256]{1,2,0:T(8,128)(2,1)S(1)} all-to-all(bf16[8,128,256]{1,2,0:T(8,128)(2,1)} %bitcast.78), channel_id=1, replica_groups=mesh['grp'=4,'wide'=8] {'wide'}, dimensions={0} | all-to-all | bytes 1048576 | tf_op jit(solution)/shard_map/all_to_all | solution.py:94
  130.1 0.2 copy.35
  130.3 11.2 %all_to_all.81 = bf16[4,256,256]{2,1,0:T(8,128)(2,1)S(1)} all-to-all(bf16[4,256,256]{2,1,0:T(8,128)(2,1)S(1)} %bitcast.74), channel_id=1, replica_groups=mesh['grp'=4,'wide'=8] {'grp'}, dimensions={0} | all-to-all | bytes 1048576 | tf_op jit(solution)/shard_map/all_to_all | solution.py:93
  141.6 1.1 convert_bitcast_fusion
  142.6 1.6 %copy.36 = f32[256,4,256]{0,2,1:T(8,128)S(1)} copy(f32[256,4,256]{2,0,1:T(8,128)} %convert_bitcast_fusion) | data formatting | bytes 2097152 | tf_op jit(solution)/shard_map/convert_element_type | solution.py:21
  144.2 0.2 multiply_reduce_fusion
  144.4 0.2 multiply_convert_fusion
  144.6 0.2 copy-done.4
  144.9 1.3 convolution_bitcast_fusion
  (23 shorter events, 0.1 us)
Async XLA Ops:
  6.5 138.1 %copy-start = (bf16[1024,512]{1,0:T(8,128)(2,1)S(1)}, bf16[1024,512]{1,0:T(8,128)(2,1)}, u32[]{:S(2)}) copy-start(bf16[1024,512]{1,0:T(8,128)(2,1)} %param.18) | copy-start | bytes 3145732
  6.5 28.6 %all-gather.3.cloned.1.call-start = ((), (), s32[]{:S(2)}) async-start(), calls=%async_computation.6 | async-start | bytes 2621440 | tf_op jit(solution)/shard_map/all_gather | solution.py:45
  7.3 55.5 %all-gather.5.cloned.1.call-start = ((), (), s32[]{:S(2)}) async-start(), calls=%async_computation.7 | async-start | bytes 2621440 | tf_op jit(solution)/shard_map/all_gather | solution.py:44
  8.0 27.2 %copy-start.1 = (bf16[128,1024]{1,0:T(8,128)(2,1)S(1)}, bf16[128,1024]{1,0:T(8,128)(2,1)}, u32[]{:S(2)}) copy-start(bf16[128,1024]{1,0:T(8,128)(2,1)} %param.11) | copy-start | bytes 786436
  24.2 20.0 %all-to-all-start.2 = ((bf16[8,128,256]{2,1,0:T(8,128)(2,1)}), bf16[8,128,256]{2,1,0:T(8,128)(2,1)S(1)}, u32[]{:S(2)}, u32[]{:S(2)}) async-start(bf16[8,128,256]{2,1,0:T(8,128)(2,1)} %bitcast.6), calls=%async_computation.2 | async-start | bytes 1048576 | tf_op jit(solution)/shard_map/all_to_all | solution.py:57
  44.2 24.8 %copy-start.3 = (s32[8,4]{0,1:T(4,128)S(1)}, s32[8,4]{0,1:T(4,128)}, u32[]{:S(2)}) copy-start(s32[8,4]{0,1:T(4,128)} %param.15) | copy-start | bytes 388
  44.2 24.9 %copy-start.5 = (s32[8]{0:T(128)S(1)}, s32[8]{0:T(128)}, u32[]{:S(2)}) copy-start(s32[8]{0:T(128)} %param.16) | copy-start | bytes 100
  44.2 21.4 %all-to-all-start = ((bf16[128,4,256]{0,2,1:T(8,128)(2,1)}), bf16[128,4,256]{0,2,1:T(8,128)(2,1)S(1)}, u32[]{:S(2)}, u32[]{:S(2)}) async-start(bf16[128,4,256]{0,2,1:T(8,128)(2,1)} %bitcast.1), calls=%async_computation | async-start | bytes 524288 | tf_op jit(solution)/shard_map/all_to_all | solution.py:55
  65.6 9.4 %all-to-all-start.3 = ((bf16[128,4,256]{0,2,1:T(8,128)(2,1)}), bf16[128,4,256]{0,2,1:T(8,128)(2,1)S(1)}, u32[]{:S(2)}, u32[]{:S(2)}) async-start(bf16[128,4,256]{0,2,1:T(8,128)(2,1)} %bitcast.8), calls=%async_computation.3 | async-start | bytes 524288 | tf_op jit(solution)/shard_map/all_to_all | solution.py:54
  142.6 1.8 %copy-start.2 = (f32[1024]{0:T(1024)S(1)}, f32[1024]{0:T(1024)}, u32[]{:S(2)}) copy-start(f32[1024]{0:T(1024)} %param.17) | copy-start | bytes 12292
  144.2 0.7 copy-start.4
Sparse Core Ops, SparseCore 0:
  8.9 26.2 all-gather.2
  36.7 25.9 all-gather.4
where the time goes:
time: 154 us; the launch traced here: 153 us
  blocking collectives  44.9 us (29%)
  waiting for transfers between devices  32.6 us (21%)
  local copies, waits for them, and re-layouts  21.7 us (14%)
  matrix products  19.4 us (13%)
  between operations  13.5 us (9%)
  starting transfers between devices  13.1 us (9%)
  other arithmetic  7.74 us (5%)
    all_to_all x1, blocking collectives, body(): lax.all_to_all(attended, 'wide', split_axis=0, concat_axis=0, tiled=True)  19.8 us
    all_gather x1, waiting for transfers between devices, body(): lax.all_gather(key_weight, 'grp', axis=1, tiled=True)  15 us
    all_to_all x1, blocking collectives, body(): lax.all_to_all(panel_query, 'grp', split_axis=1, concat_axis=0, tiled=True)  13.9 us
    all_to_all x1, blocking collectives, body(): lax.all_to_all(lax.all_to_all(attended, 'wide', split_axis=0, concat_axis...  11.2 us
    dot_general x2, matrix products, attend(): jnp.einsum('bhij,bjhd->bihd', weights, picked_values, preferred_element_t...  9.29 us
    gather x2, local copies, waits for them, and re-layouts, attend(): key_blocks[listed].reshape(per_step, LMAX * BLK, local_heads, HD)  7.12 us
    gather x2, local copies, waits for them, and re-layouts, attend(): value_blocks[listed].reshape(per_step, LMAX * BLK, local_heads, HD)  7.11 us
    all_to_all x1, waiting for transfers between devices, body(): lax.all_to_all(lax.all_to_all(panel_query, 'grp', split_axis=1, concat_ax...  6.16 us
  transfers between devices with their start and end apart: 5, of which 4 were waited for; matrix products, arithmetic and copies ran while one was open for 6% of the time, Pallas kernels for 0%

commit v1 on v0

v1 whole, which is shorter than its diff:
```python
import functools
import math

import jax
import jax.numpy as jnp
from jax import lax
from jax.experimental import pallas as pl
from jax.experimental.pallas import tpu as pltpu
from jax.sharding import PartitionSpec as P

BLK = 128
LMAX = 4
HD = 64
LANES = 128
MESH = pl.DeviceIdType.MESH


def flip(index, bits):
    bit = 1
    while bit <= bits:
        if bits & bit:
            index = index + bit * (1 - 2 * ((index // bit) % 2))
        bit *= 2
    return index


def kernel(
    n_wide,
    n_grp,
    anchor_hbm,
    key_hbm,
    value_hbm,
    query_hbm,
    list_ref,
    count_ref,
    gain_ref,
    up_hbm,
    flux_w_ref,
    flux_ref,
    anchors,
    weights,
    keys,
    values,
    region_query,
    outgoing,
    attended,
    query,
    up,
    local_sem,
    anchor_send,
    anchor_recv,
    forward_send,
    query_send,
    query_recv,
    out_send,
    out_recv,
):
    w = lax.axis_index("wide")
    g = lax.axis_index("grp")
    slabs = n_wide // n_grp
    slab = region_query.shape[1]
    cols = region_query.shape[2]
    pairs = cols // LANES
    chips = n_grp // 2
    core = g % 2
    chip = g // 2
    sibling = chip * 2 + 1 - core
    home = w // slabs
    here = home == g

    loads = [
        pltpu.make_async_copy(anchor_hbm, anchors.at[g], local_sem.at[0]),
        pltpu.make_async_copy(key_hbm, weights.at[:, pl.ds(0, cols)], local_sem.at[1]),
        pltpu.make_async_copy(value_hbm, weights.at[:, pl.ds(cols, cols)], local_sem.at[2]),
        pltpu.make_async_copy(query_hbm, query, local_sem.at[3]),
        pltpu.make_async_copy(up_hbm, up, local_sem.at[4]),
    ]
    for load in loads:
        load.start()

    barrier = pltpu.get_barrier_semaphore()

    def greet(wide, grp):
        pl.semaphore_signal(barrier, inc=1, device_id=(grp, wide), device_id_type=MESH)

    @pl.loop(1, n_grp)
    def _(i):
        greet(w, (g + i) % n_grp)

    @pl.loop(0, n_wide)
    def _(i):
        region = g * slabs + i // n_grp
        head = i % n_grp

        @pl.when(jnp.logical_or(region != w, head != g))
        def _():
            greet(region, head)

        @pl.when(jnp.logical_or(i != w, home != g))
        def _():
            greet(i, home)

    pl.semaphore_wait(barrier, n_grp - 1 + 2 * n_wide - 2 * here.astype(jnp.int32))

    def anchor_copy(grp, index):
        return pltpu.make_async_remote_copy(
            src_ref=anchor_hbm,
            dst_ref=anchors.at[g],
            send_sem=anchor_send.at[index],
            recv_sem=anchor_recv.at[g],
            device_id=(grp, w),
            device_id_type=MESH,
        )

    for j in range(1, chips):
        anchor_copy(((chip + j) % chips) * 2 + core, j).start()
    anchor_copy(sibling, 0).start()

    def query_source(i):
        s = i // n_grp
        head = i % n_grp
        return query_hbm.at[
            pl.ds(pl.multiple_of(s * slab, 16), slab), pl.ds(pl.multiple_of(head * cols, LANES), cols)
        ]

    def query_copy(i):
        return pltpu.make_async_remote_copy(
            src_ref=query_source(i),
            dst_ref=region_query.at[w],
            send_sem=query_send.at[i],
            recv_sem=query_recv.at[w],
            device_id=(i % n_grp, g * slabs + i // n_grp),
            device_id_type=MESH,
        )

    def is_self(i):
        return jnp.logical_and(g * slabs + i // n_grp == w, i % n_grp == g)

    @pl.loop(0, n_wide)
    def _(i):
        @pl.when(is_self(i))
        def _():
            pltpu.make_async_copy(query_source(i), region_query.at[w], query_recv.at[w]).start()

        @pl.when(jnp.logical_not(is_self(i)))
        def _():
            query_copy(i).start()

    low = lax.broadcasted_iota(jnp.int32, (BLK, LANES), 1) < HD

    def project(cell):
        both = jnp.dot(anchors[cell], weights[...], preferred_element_type=jnp.float32)
        rows = pl.ds(pl.multiple_of(cell * BLK, BLK), BLK)
        for j in range(pairs):
            k = both[:, j * LANES : (j + 1) * LANES]
            v = both[:, cols + j * LANES : cols + (j + 1) * LANES]
            keys[j, 0, rows, :] = jnp.where(low, k, 0.0).astype(jnp.bfloat16)
            keys[j, 1, rows, :] = jnp.where(low, 0.0, k).astype(jnp.bfloat16)
            values[j, 0, rows, :] = jnp.where(low, v, 0.0).astype(jnp.bfloat16)
            values[j, 1, rows, :] = jnp.where(low, 0.0, v).astype(jnp.bfloat16)

    def wait_anchor(cell):
        pltpu.make_async_copy(anchors.at[cell], anchors.at[cell], anchor_recv.at[cell]).wait()

    def forward_copy(cell, j):
        return pltpu.make_async_remote_copy(
            src_ref=anchors.at[cell],
            dst_ref=anchors.at[cell],
            send_sem=forward_send.at[j],
            recv_sem=anchor_recv.at[cell],
            device_id=(sibling, w),
            device_id_type=MESH,
        )

    def across(j):
        return (chip + chips - j) % chips

    for load in loads[:3]:
        load.wait()
    project(g)
    wait_anchor(sibling)
    project(sibling)
    for j in range(1, chips):
        cell = across(j) * 2 + core
        wait_anchor(cell)
        forward_copy(cell, j).start()
        project(cell)
    for j in range(1, chips):
        cell = across(j) * 2 + 1 - core
        wait_anchor(cell)
        project(cell)

    scale = math.log2(math.e) / math.sqrt(HD)
    first = lax.broadcasted_iota(jnp.int32, (slab, LANES), 1) < HD
    nt = (((1,), (1,)), ((), ()))

    def out_copy(p):
        return pltpu.make_async_remote_copy(
            src_ref=outgoing.at[p],
            dst_ref=attended.at[g, w % slabs],
            send_sem=out_send.at[p],
            recv_sem=out_recv.at[g, w % slabs],
            device_id=(home, p),
            device_id_type=MESH,
        )

    def attend(p):
        block = p * slab // BLK
        used = count_ref[block]
        bias = []
        for c in range(n_grp):
            live = jnp.logical_and(list_ref[0, block] == c, used > 0)
            for slot in range(1, LMAX):
                live = jnp.logical_or(live, jnp.logical_and(list_ref[slot, block] == c, used > slot))
            bias.append(jnp.full((1, BLK), jnp.where(live, 0.0, -jnp.inf), jnp.float32))
        bias = jnp.concatenate(bias, axis=1)
        pltpu.make_async_copy(region_query.at[p], region_query.at[p], query_recv.at[p]).wait()
        for j in range(pairs):
            q = region_query[p, :, j * LANES : (j + 1) * LANES]
            total = None
            sums = []
            for i in range(2):
                scores = lax.dot_general(q, keys[j, i], nt, preferred_element_type=jnp.float32)
                scores = scores * scale + bias
                top = jnp.max(scores, axis=-1, keepdims=True)
                expo = jnp.exp2(scores - top)
                sums.append(jnp.sum(expo, axis=-1, keepdims=True))
                part = jnp.dot(
                    expo.astype(jnp.bfloat16), values[j, i], preferred_element_type=jnp.float32
                )
                total = part if total is None else total + part
            inverse = jnp.where(first, 1.0 / sums[0], 1.0 / sums[1])
            outgoing[p, :, j * LANES : (j + 1) * LANES] = (total * inverse).astype(jnp.bfloat16)

    @pl.loop(0, n_wide)
    def _(k):
        p = w
        bit = 1
        while bit < n_wide:
            step = (k // bit) % 2
            p = p + step * bit * (1 - 2 * ((p // bit) % 2))
            bit *= 2
        attend(p)
        mine = jnp.logical_and(p == w, here)

        @pl.when(mine)
        def _():
            pltpu.make_async_copy(
                outgoing.at[p], attended.at[g, w % slabs], out_recv.at[g, w % slabs]
            ).start()

        @pl.when(jnp.logical_not(mine))
        def _():
            out_copy(p).start()

    for load in loads[3:]:
        load.wait()
    for h in range(n_grp):
        for s in range(slabs):
            pltpu.make_async_copy(
                attended.at[h, s], attended.at[h, s], out_recv.at[h, s]
            ).wait()
    rows = query.shape[0]
    dim = query.shape[1]
    stream = []
    square = jnp.zeros((rows, 1), jnp.float32)
    for h in range(n_grp):
        part = query[:, h * cols : (h + 1) * cols].astype(jnp.float32) + attended[h].reshape(
            rows, cols
        ).astype(jnp.float32)
        square = square + jnp.sum(part * part, axis=-1, keepdims=True)
        stream.append(part)
    factor = lax.rsqrt(square / dim + 1e-06)
    normed = jnp.concatenate(
        [
            (stream[h] * factor * gain_ref[:, h * cols : (h + 1) * cols]).astype(jnp.bfloat16)
            for h in range(n_grp)
        ],
        axis=1,
    )
    hidden = jax.nn.gelu(
        jnp.dot(normed, up[...], preferred_element_type=jnp.float32), approximate=True
    ).astype(jnp.bfloat16)
    flux_ref[...] = lax.dot_general(flux_w_ref[...], hidden, nt, preferred_element_type=jnp.float32)

    for j in range(1, chips):
        anchor_copy(((chip + j) % chips) * 2 + core, j).wait_send()
        forward_copy(across(j) * 2 + core, j).wait_send()
    anchor_copy(sibling, 0).wait_send()

    @pl.loop(0, n_wide)
    def _(i):
        @pl.when(jnp.logical_not(is_self(i)))
        def _():
            query_copy(i).wait_send()

        @pl.when(jnp.logical_not(jnp.logical_and(i == w, here)))
        def _():
            out_copy(i).wait_send()


def body(n_wide, n_grp, anchor, key_w, value_w, query, cell_list, cell_count, gain, up, flux_w):
    rows, dim = query.shape
    cols = key_w.shape[1]
    slabs = n_wide // n_grp
    slab = rows // slabs
    cells = n_grp
    pairs = cols // LANES
    any_space = pl.BlockSpec(memory_space=pl.ANY)
    vmem = pl.BlockSpec(memory_space=pltpu.VMEM)
    smem = pl.BlockSpec(memory_space=pltpu.SMEM)
    bf16 = jnp.bfloat16
    dma = pltpu.SemaphoreType.DMA
    return pl.pallas_call(
        functools.partial(kernel, n_wide, n_grp),
        out_shape=jax.ShapeDtypeStruct((flux_w.shape[0], rows), jnp.float32),
        in_specs=[any_space] * 4 + [smem] * 2 + [vmem, any_space, vmem],
        out_specs=vmem,
        scratch_shapes=[
            pltpu.VMEM((cells, BLK, dim), bf16),
            pltpu.VMEM((dim, 2 * cols), bf16),
            pltpu.VMEM((pairs, 2, cells * BLK, LANES), bf16),
            pltpu.VMEM((pairs, 2, cells * BLK, LANES), bf16),
            pltpu.VMEM((n_wide, slab, cols), bf16),
            pltpu.VMEM((n_wide, slab, cols), bf16),
            pltpu.VMEM((n_grp, slabs, slab, cols), bf16),
            pltpu.VMEM((rows, dim), bf16),
            pltpu.VMEM(up.shape, bf16),
            dma((5,)),
            dma((max(n_grp // 2, 1),)),
            dma((n_grp,)),
            dma((max(n_grp // 2, 1),)),
            dma((n_wide,)),
            dma((n_wide,)),
            dma((n_wide,)),
            dma((n_grp, slabs)),
        ],
        compiler_params=pltpu.CompilerParams(
            collective_id=0, has_side_effects=True, vmem_limit_bytes=56 * 1024 * 1024
        ),
        cost_estimate=pl.CostEstimate(flops=3 * 10**9, bytes_accessed=6 * 10**6, transcendentals=0),
    )(anchor, key_w, value_w, query, cell_list.T, cell_count, gain[None, :], up, flux_w)


def solution(mesh):
    in_specs = (
        P(("wide", "grp"), None),
        P(None, "grp"),
        P(None, "grp"),
        P(("wide", "grp"), None),
        P("wide", None),
        P("wide"),
        P(),
        P(),
        P(),
    )
    out_specs = P(None, ("wide", "grp"))
    step = functools.partial(body, mesh.shape["wide"], mesh.shape["grp"])
    return jax.shard_map(step, mesh=mesh, in_specs=in_specs, out_specs=out_specs, check_vma=False)
```

time: 154 us -> 47.4 us (0.31)
  the two profiles are of different devices: /device:TPU:0 before, /device:TPU:17 now
where the time goes in v1:
time: 47.4 us; the launch traced here: 47.2 us
  Pallas kernels  45.9 us (97%)
  local copies, waits for them, and re-layouts  1.28 us (3%)
    pallas_call x1, Pallas kernels, body(): pl.pallas_call(functools.partial(kernel, n_wide, n_grp), out_shape=jax.Sh...  45.9 us
    unnamed x1, local copies, waits for them, and re-layouts  1.28 us

profile of v1, /device:TPU:17, one launch (start us, length us, event | category | flops | bytes accessed | tf_op | source)
XLA Modules:
  0.0 47.2 jit_solution(13917346734199676451)
XLA Ops:
  0.0 45.9 %shard_map.91 = f32[4,256]{1,0:T(4,128)} custom-call(bf16[128,1024]{1,0:T(8,128)(2,1)} %anchor_hbm.1, bf16[1024,256]{1,0:T(8,128)(2,1)} %key_hbm.1, bf16[1024,256]{1,0:T(8,128)(2,1)} %value_hbm.1, bf16[256,1024]{1,0:T(8,128)(2,1)} %query_hbm.1, s32[4,8]{1,0:T(4,128)} %bitcast.3, s32[8]{0:T(128)} %count_ref.1, f32[1,1024]{1,0:T(1,128)} %bitcast.2, ...), custom_call_target="tpu_custom_call" | custom-call | flops 3000000000 | bytes 6000000 | tf_op jit(solution)/shard_map/pallas_call | solution.py:314
  45.9 1.3 %copy.11 = f32[4,256]{1,0:T(4,128)} copy(f32[4,256]{1,0:T(4,128)} %shard_map.91) | data formatting | bytes 8192

commit v2 on v1

--- a/solution.py
+++ b/solution.py
@@ -13,15 +13,6 @@
 HD = 64
 LANES = 128
 MESH = pl.DeviceIdType.MESH
-
-
-def flip(index, bits):
-    bit = 1
-    while bit <= bits:
-        if bits & bit:
-            index = index + bit * (1 - 2 * ((index // bit) % 2))
-        bit *= 2
-    return index
 
 
 def kernel(
@@ -46,6 +37,8 @@
     attended,
     query,
     up,
+    relay,
+    back,
     local_sem,
     anchor_send,
     anchor_recv,
@@ -54,6 +47,10 @@
     query_recv,
     out_send,
     out_recv,
+    relay_send,
+    relay_recv,
+    back_send,
+    back_recv,
 ):
     w = lax.axis_index("wide")
     g = lax.axis_index("grp")
@@ -87,20 +84,12 @@
     def _(i):
         greet(w, (g + i) % n_grp)
 
-    @pl.loop(0, n_wide)
+    @pl.loop(1, n_wide)
     def _(i):
-        region = g * slabs + i // n_grp
-        head = i % n_grp
-
-        @pl.when(jnp.logical_or(region != w, head != g))
-        def _():
-            greet(region, head)
-
-        @pl.when(jnp.logical_or(i != w, home != g))
-        def _():
-            greet(i, home)
-
-    pl.semaphore_wait(barrier, n_grp - 1 + 2 * n_wide - 2 * here.astype(jnp.int32))
+        greet((w + i) % n_wide, g)
+        greet((w + i) % n_wide, sibling)
+
+    pl.semaphore_wait(barrier, n_grp - 1 + 2 * (n_wide - 1))
 
     def anchor_copy(grp, index):
         return pltpu.make_async_remote_copy(
@@ -116,35 +105,96 @@
         anchor_copy(((chip + j) % chips) * 2 + core, j).start()
     anchor_copy(sibling, 0).start()
 
-    def query_source(i):
-        s = i // n_grp
-        head = i % n_grp
+    def query_source(s, head):
         return query_hbm.at[
             pl.ds(pl.multiple_of(s * slab, 16), slab), pl.ds(pl.multiple_of(head * cols, LANES), cols)
         ]
 
-    def query_copy(i):
-        return pltpu.make_async_remote_copy(
-            src_ref=query_source(i),
+    def direct_copy(s, head):
+        return pltpu.make_async_remote_copy(
+            src_ref=query_source(s, head),
             dst_ref=region_query.at[w],
-            send_sem=query_send.at[i],
+            send_sem=query_send.at[s * n_grp + head],
             recv_sem=query_recv.at[w],
-            device_id=(i % n_grp, g * slabs + i // n_grp),
-            device_id_type=MESH,
-        )
-
-    def is_self(i):
-        return jnp.logical_and(g * slabs + i // n_grp == w, i % n_grp == g)
-
-    @pl.loop(0, n_wide)
-    def _(i):
-        @pl.when(is_self(i))
-        def _():
-            pltpu.make_async_copy(query_source(i), region_query.at[w], query_recv.at[w]).start()
-
-        @pl.when(jnp.logical_not(is_self(i)))
-        def _():
-            query_copy(i).start()
+            device_id=(head, g * slabs + s),
+            device_id_type=MESH,
+        )
+
+    def relay_index(j, from_core, s):
+        return ((j - 1) * 2 + from_core) * slabs + s
+
+    def relayed_copy(j, s, head):
+        index = relay_index(j, core, s)
+        return pltpu.make_async_remote_copy(
+            src_ref=query_source(s, head),
+            dst_ref=relay.at[index],
+            send_sem=query_send.at[s * n_grp + head],
+            recv_sem=relay_recv.at[index],
+            device_id=(head, w),
+            device_id_type=MESH,
+        )
+
+    def each_query(act_relayed, act_direct, act_self):
+        for j in range(1, chips):
+            for c in range(2):
+                head = ((chip + j) % chips) * 2 + c
+
+                @pl.loop(0, slabs)
+                def _(s):
+                    same = g * slabs + s == w
+
+                    @pl.when(same)
+                    def _():
+                        act_direct(s, head)
+
+                    @pl.when(jnp.logical_not(same))
+                    def _():
+                        act_relayed(j, s, head)
+
+        @pl.loop(0, slabs)
+        def _(s):
+            act_direct(s, sibling)
+            same = g * slabs + s == w
+
+            @pl.when(same)
+            def _():
+                act_self(s)
+
+            @pl.when(jnp.logical_not(same))
+            def _():
+                act_direct(s, g)
+
+    each_query(
+        lambda j, s, head: relayed_copy(j, s, head).start(),
+        lambda s, head: direct_copy(s, head).start(),
+        lambda s: pltpu.make_async_copy(
+            query_source(s, g), region_query.at[w], query_recv.at[w]
+        ).start(),
+    )
+
+    def forward_query(j, c, s):
+        index = relay_index(j, c, s)
+        source = ((chip + chips - j) % chips) * 2 + c
+        return pltpu.make_async_remote_copy(
+            src_ref=relay.at[index],
+            dst_ref=region_query.at[w],
+            send_sem=relay_send.at[index],
+            recv_sem=query_recv.at[w],
+            device_id=(g, source * slabs + s),
+            device_id_type=MESH,
+        )
+
+    def each_relay(act):
+        for j in range(1, chips):
+            for c in range(2):
+
+                @pl.loop(0, slabs)
+                def _(s):
+                    source = ((chip + chips - j) % chips) * 2 + c
+
+                    @pl.when(source * slabs + s != w)
+                    def _():
+                        act(j, c, s)
 
     low = lax.broadcasted_iota(jnp.int32, (BLK, LANES), 1) < HD
 
@@ -190,6 +240,13 @@
         wait_anchor(cell)
         project(cell)
 
+    def pass_on(j, c, s):
+        index = relay_index(j, c, s)
+        pltpu.make_async_copy(relay.at[index], relay.at[index], relay_recv.at[index]).wait()
+        forward_query(j, c, s).start()
+
+    each_relay(pass_on)
+
     scale = math.log2(math.e) / math.sqrt(HD)
     first = lax.broadcasted_iota(jnp.int32, (slab, LANES), 1) < HD
     nt = (((1,), (1,)), ((), ()))
@@ -203,6 +260,38 @@
             device_id=(home, p),
             device_id_type=MESH,
         )
+
+    def hop_copy(p):
+        return pltpu.make_async_remote_copy(
+            src_ref=outgoing.at[p],
+            dst_ref=back.at[w],
+            send_sem=out_send.at[p],
+            recv_sem=back_recv.at[w],
+            device_id=(g, p),
+            device_id_type=MESH,
+        )
+
+    def back_copy(r):
+        return pltpu.make_async_remote_copy(
+            src_ref=back.at[r],
+            dst_ref=attended.at[g, r % slabs],
+            send_sem=back_send.at[r],
+            recv_sem=out_recv.at[g, r % slabs],
+            device_id=(r // slabs, w),
+            device_id_type=MESH,
+        )
+
+    def straight(p):
+        return jnp.logical_or(home // 2 == chip, p == w)
+
+    def flipped(k):
+        p = w
+        bit = 1
+        while bit < n_wide:
+            step = (k // bit) % 2
+            p = p + step * bit * (1 - 2 * ((p // bit) % 2))
+            bit *= 2
+        return p
 
     def attend(p):
         block = p * slab // BLK
@@ -234,12 +323,7 @@
 
     @pl.loop(0, n_wide)
     def _(k):
-        p = w
-        bit = 1
-        while bit < n_wide:
-            step = (k // bit) % 2
-            p = p + step * bit * (1 - 2 * ((p // bit) % 2))
-            bit *= 2
+        p = flipped(k)
         attend(p)
         mine = jnp.logical_and(p == w, here)
 
@@ -249,9 +333,22 @@
                 outgoing.at[p], attended.at[g, w % slabs], out_recv.at[g, w % slabs]
             ).start()
 
-        @pl.when(jnp.logical_not(mine))
+        @pl.when(jnp.logical_and(straight(p), jnp.logical_not(mine)))
         def _():
             out_copy(p).start()
+
+        @pl.when(jnp.logical_not(straight(p)))
+        def _():
+            hop_copy(p).start()
+
+    @pl.loop(1, n_wide)
+    def _(k):
+        r = flipped(k)
+
+        @pl.when((r // slabs) // 2 != chip)
+        def _():
+            pltpu.make_async_copy(back.at[r], back.at[r], back_recv.at[r]).wait()
+            back_copy(r).start()
 
     for load in loads[3:]:
         load.wait()
@@ -288,15 +385,22 @@
         forward_copy(across(j) * 2 + core, j).wait_send()
     anchor_copy(sibling, 0).wait_send()
 
+    each_query(
+        lambda j, s, head: relayed_copy(j, s, head).wait_send(),
+        lambda s, head: direct_copy(s, head).wait_send(),
+        lambda s: None,
+    )
+    each_relay(lambda j, c, s: forward_query(j, c, s).wait_send())
+
     @pl.loop(0, n_wide)
     def _(i):
-        @pl.when(jnp.logical_not(is_self(i)))
-        def _():
-            query_copy(i).wait_send()
-
         @pl.when(jnp.logical_not(jnp.logical_and(i == w, here)))
         def _():
             out_copy(i).wait_send()
+
+        @pl.when(jnp.logical_and(i != w, (i // slabs) // 2 != chip))
+        def _():
+            back_copy(i).wait_send()
 
 
 def body(n_wide, n_grp, anchor, key_w, value_w, query, cell_list, cell_count, gain, up, flux_w):
@@ -326,6 +430,8 @@
             pltpu.VMEM((n_grp, slabs, slab, cols), bf16),
             pltpu.VMEM((rows, dim), bf16),
             pltpu.VMEM(up.shape, bf16),
+            pltpu.VMEM((max(n_grp - 2, 1) * slabs, slab, cols), bf16),
+            pltpu.VMEM((n_wide, slab, cols), bf16),
             dma((5,)),
             dma((max(n_grp // 2, 1),)),
             dma((n_grp,)),
@@ -334,6 +440,10 @@
             dma((n_wide,)),
             dma((n_wide,)),
             dma((n_grp, slabs)),
+            dma((max(n_grp - 2, 1) * slabs,)),
+            dma((max(n_grp - 2, 1) * slabs,)),
+            dma((n_wide,)),
+            dma((n_wide,)),
         ],
         compiler_params=pltpu.CompilerParams(
             collective_id=0, has_side_effects=True, vmem_limit_bytes=56 * 1024 * 1024

time: 47.4 us -> 50.6 us (1.068)
  the two profiles are of different devices: /device:TPU:17 before, /device:TPU:3 now
where the time goes in v2:
time: 50.6 us; the launch traced here: 50.4 us
  Pallas kernels  49.1 us (97%)
  local copies, waits for them, and re-layouts  1.28 us (3%)
    pallas_call x1, Pallas kernels, body(): pl.pallas_call(functools.partial(kernel, n_wide, n_grp), out_shape=jax.Sh...  49.1 us
    unnamed x1, local copies, waits for them, and re-layouts  1.28 us

profile of v2, /device:TPU:3, one launch (start us, length us, event | category | flops | bytes accessed | tf_op | source)
XLA Modules:
  0.0 50.4 jit_solution(15841912824466449283)
XLA Ops:
  0.0 49.1 %shard_map.91 = f32[4,256]{1,0:T(4,128)} custom-call(bf16[128,1024]{1,0:T(8,128)(2,1)} %anchor_hbm.1, bf16[1024,256]{1,0:T(8,128)(2,1)} %key_hbm.1, bf16[1024,256]{1,0:T(8,128)(2,1)} %value_hbm.1, bf16[256,1024]{1,0:T(8,128)(2,1)} %query_hbm.1, s32[4,8]{1,0:T(4,128)} %bitcast.3, s32[8]{0:T(128)} %count_ref.1, f32[1,1024]{1,0:T(1,128)} %bitcast.2, ...), custom_call_target="tpu_custom_call" | custom-call | flops 3000000000 | bytes 6000000 | tf_op jit(solution)/shard_map/pallas_call | solution.py:418
  49.1 1.3 %copy.11 = f32[4,256]{1,0:T(4,128)} copy(f32[4,256]{1,0:T(4,128)} %shard_map.91) | data formatting | bytes 8192
